TPU v7x, 32 devices: a whole 2x2x4 slice. The times are simulated.
32 devices in a mesh: groups: 2 (over y), clus: 4 (over z), pair: 2 (over x), rhs: 2 (over core).
Axes of the slice: x: 2, y: 2, z: 4, core: 2. Of those that a mesh axis runs over, the one named last changes fastest.
Arguments:
- rhs_field: float32 [16, 16384], P('rhs', ('groups', 'clus')), parts along dimension 1, may hold values from -6 to 6
- coefficients: float32 [4], replicated, may hold values from -1 to 1
- near_blocks: bfloat16 [256, 256, 256], P(('groups', 'clus', 'pair')), parts along dimension 0, may hold values from -0.125 to 0.125
- near_tgt: int32 [256], P(('groups', 'clus', 'pair')), parts along dimension 0, may hold values from 0 to 31, as said below
- near_src: int32 [256], P(('groups', 'clus', 'pair')), parts along dimension 0, may hold values from 0 to 31, as said below
- row_basis: bfloat16 [64, 16, 256], P(('groups', 'clus')), parts along dimension 0, may hold values from -0.25 to 0.25
- col_basis: bfloat16 [1024, 16, 256], P(('groups', 'clus', 'pair')), parts along dimension 0, may hold values from -0.375 to 0.375
- far_src: int32 [1024], P(('groups', 'clus', 'pair')), parts along dimension 0, may hold values from 0 to 31, as said below
- far_tgt: int32 [1024], P(('groups', 'clus', 'pair')), parts along dimension 0, may hold values from 0 to 31, as said below
Outputs:
- preconditioned: float32 [16, 16384], P('rhs', ('groups', 'clus')), parts along dimension 1
There are 2 independent parts, one for each index of `groups`. A program takes and returns all parts, laid end to end along the dimension named above; an argument that names none is the same for every part. Nothing has to cross between parts.
Inputs may be any that keep to these rules, and one draw needn't show every extreme that they name: `near_tgt`: the rows are in aligned blocks of 16, one a device in the order of clus then pair; the block of clus index c names clusters c * 8 to (c + 1) * 8 - 1. `near_src`: in each aligned block of 16 rows (one a device, clus then pair, clus index c), exactly 2 rows name clusters of clus index c - 1 and exactly 2 name clusters of clus index c + 1 (both taken modulo the number of clus indices; cluster // 8 is a cluster's clus index), and all others name clusters of clus index c. `far_src`: the rows are in aligned blocks of 64, one a device in the order of clus then pair; the block of clus index c names clusters c * 8 to (c + 1) * 8 - 1. `far_tgt`: never equal to far_src of the same row.
All inputs are finite; a program needn't handle non-finite values.
Results may differ from a plain program's by a relative error of at most 0.0047.
Values may be sent and summed in bfloat16 or wider, within the bound.
A program may use at most 64 MiB of HBM per device.

v0:
```python
import functools

import jax
import jax.numpy as jnp
from jax import lax
from jax.experimental import pallas as pl
from jax.experimental.pallas import tpu as pltpu
from jax.sharding import PartitionSpec as P

MESH = pl.DeviceIdType.MESH
F32 = jnp.float32
BF16 = jnp.bfloat16
CAP = 2
LANES = 128
NEAR_UNROLL = 4
WIRE = BF16


def drain(buffer, sem):
    pltpu.make_async_copy(buffer, buffer, sem).wait()


def split(value):
    high = value.astype(BF16)
    return high, (value - high.astype(F32)).astype(BF16)


def kernel(
    sizes, coeff_h, near_tgt_h, near_src_h, far_src_h, far_tgt_h, rhs_h, near_h, row_h, col_h, out,
    coeff, near_tgt, near_src, far_src, far_tgt, rhs, near_v, row_v, col_v,
    xs, x0_send, x0_recv, x0_wide, rq_send, rq_recv,
    src_lane, held, fold, s_send, s_recv, n_send, n_recv, sel_send, sel_recv, index_s,
    load_sem, x0_sems, rq_sems, s_sems, n_sems, sel_sems,
):
    clus, pairs, clusters, rows, leaf, rank, near_count, far_count, degree_top = sizes
    group = clus * pairs
    chunk = clusters * rank
    c = lax.axis_index("clus")
    p = lax.axis_index("pair")
    me = c * pairs + p
    up = lax.rem(c + 1, clus)
    down = lax.rem(c + clus - 1, clus)
    base = c * clusters
    beside = (down, up)

    places = (
        (coeff_h, coeff), (rhs_h, rhs), (far_tgt_h, far_tgt), (far_src_h, far_src), (near_src_h, near_src),
        (near_tgt_h, near_tgt), (col_h, col_v), (row_h, row_v), (near_h, near_v),
    )
    loads = [pltpu.make_async_copy(src, dst, load_sem.at[i]) for i, (src, dst) in enumerate(places)]
    for load in loads:
        load.start()

    def each(first, count, body):
        if count - first <= 2:
            for i in range(first, count):
                body(i)
        else:
            lax.fori_loop(first, count, lambda i, x: (body(i), x)[1], 0)

    def peer(d):
        other = lax.rem(me + d, group)
        return {"clus": lax.div(other, pairs), "pair": lax.rem(other, pairs)}

    barrier = pltpu.get_barrier_semaphore()
    each(1, group, lambda d: pl.semaphore_signal(barrier, inc=1, device_id=peer(d), device_id_type=MESH))

    def send(src, dst, send_sem, recv_sem, device):
        pltpu.make_async_remote_copy(
            src_ref=src, dst_ref=dst, send_sem=send_sem, recv_sem=recv_sem,
            device_id=device, device_id_type=MESH,
        ).start()

    for load in loads[:6]:
        load.wait()

    scale = coeff[degree_top]
    first = [(scale * rhs[:, s * leaf : (s + 1) * leaf]).astype(BF16).astype(F32) for s in range(clusters)]
    for s in range(clusters):
        xs[s] = first[s]
    x0_send[...] = jnp.concatenate(first, axis=0).astype(BF16)

    def find(j, state):
        counts, wanted = list(state[:2]), list(state[2:])
        owner = lax.div(near_src[j], clusters)
        local = near_src[j] - owner * clusters
        place = local
        for d in range(2):
            here = owner == beside[d]
            for u in range(CAP):
                wanted[d * CAP + u] = jnp.where(here & (counts[d] == u), local, wanted[d * CAP + u])
            place = jnp.where(here, clusters + d * CAP + jnp.minimum(counts[d], CAP - 1), place)
            counts[d] = counts[d] + jnp.where(here, 1, 0)
        index_s[j] = place
        return (*counts, *wanted)

    wanted = lax.fori_loop(0, near_count, find, (jnp.int32(0),) * (2 + 2 * CAP))[2:]
    cluster_row = lax.broadcasted_iota(jnp.int32, (clusters, LANES), 0)
    for d in range(2):
        for u in range(CAP):
            rq_send[d, u * clusters : (u + 1) * clusters, :] = jnp.where(cluster_row == wanted[d * CAP + u], 1.0, 0.0)

    pl.semaphore_wait(barrier, group - 1)
    for d in range(2):
        send(x0_send, x0_recv.at[1 - d], x0_sems.at[0, d], x0_sems.at[1, 1 - d], {"clus": beside[d], "pair": p})
    for d in range(2):
        def ask(e, d=d):
            device = {"clus": beside[d], "pair": lax.rem(p + e, pairs)}
            send(rq_send.at[d], rq_recv.at[1 - d, e], rq_sems.at[0, d], rq_sems.at[1, 1 - d], device)
        each(0, pairs, ask)

    lane = lax.broadcasted_iota(jnp.int32, (rows, LANES), 1)
    per_tile = LANES // rank

    def mark_tile(q, unused):
        value = jnp.zeros((rows, LANES), jnp.int32)
        for i in range(per_tile):
            value = jnp.where(lane >= i * rank, far_src[q * per_tile + i] - base, value)
        src_lane[q] = value
        return unused

    lax.fori_loop(0, far_count // per_tile, mark_tile, 0)
    width = clus * chunk
    offset = lax.broadcasted_iota(jnp.int32, (rank, width), 1) - lax.broadcasted_iota(jnp.int32, (rank, width), 0)

    def place_block(j, unused):
        start = pl.multiple_of(j * rank, rank)
        fold[pl.ds(start, rank), :] = jnp.where(offset == far_tgt[j] * rank, 1.0, 0.0).astype(BF16)
        return unused

    lax.fori_loop(0, far_count, place_block, 0, unroll=2)
    loads[6].wait()
    loads[7].wait()

    contract_last = (((1,), (1,)), ((), ()))
    tile_lanes = far_count // per_tile

    def product(step, unused):
        degree = degree_top - 1 - step

        own = jnp.concatenate([xs[s] for s in range(clusters)], axis=0).astype(BF16)
        every = lax.dot_general(own, col_v[...], contract_last, preferred_element_type=F32)
        parts = []
        for q in range(tile_lanes):
            source_of = src_lane[q]
            total = jnp.zeros((rows, LANES), F32)
            for s in range(clusters):
                piece = every[s * rows : (s + 1) * rows, q * LANES : (q + 1) * LANES]
                total = total + jnp.where(source_of == s, piece, 0.0)
            parts.append(total)
        coef = jnp.concatenate(parts, axis=1)
        both = jnp.dot(jnp.concatenate(split(coef), axis=0), fold[...], preferred_element_type=F32)
        mine = both[:rows] + both[rows:]
        for i in range(clus):
            s_send[step, i] = mine[:, i * chunk : (i + 1) * chunk]

        def spread(d):
            there = lax.rem(c + d, clus)
            send(s_send.at[step, there], s_recv.at[step, d - 1], s_sems.at[0, step], s_sems.at[1, step],
                 {"clus": there, "pair": p})

        each(1, clus, spread)

        @pl.when(step == 0)
        def _():
            for d in range(2):
                drain(x0_recv.at[d], x0_sems.at[1, d])
                wide = x0_recv[d].astype(F32)
                for s in range(clusters):
                    x0_wide[d, s] = wide[s * rows : (s + 1) * rows]
                for u in range(CAP):
                    xs[clusters + d * CAP + u] = x0_wide[d, wanted[d * CAP + u]]
            loads[8].wait()

        @pl.when(step > 0)
        def _():
            for d in range(2):
                drain(sel_recv.at[step - 1, d], sel_sems.at[1, step - 1, d])
                value = sel_recv[step - 1, d, 0].astype(F32)
                for e in range(1, pairs):
                    value = value + sel_recv[step - 1, d, e].astype(F32)
                for u in range(CAP):
                    xs[clusters + d * CAP + u] = value[u * rows : (u + 1) * rows].astype(BF16).astype(F32)

        def near_block(i, near):
            near = list(near)
            for k in range(NEAR_UNROLL):
                j = i * NEAR_UNROLL + k
                value = lax.dot_general(
                    xs[index_s[j]].astype(BF16), near_v[j], contract_last, preferred_element_type=F32)
                target = near_tgt[j] - base
                for s in range(clusters):
                    near[s] = near[s] + value * jnp.where(target == s, 1.0, 0.0)
            return tuple(near)

        near = lax.fori_loop(
            0, near_count // NEAR_UNROLL, near_block,
            tuple(jnp.zeros((rows, leaf), F32) for s in range(clusters)))

        drain(s_recv.at[step], s_sems.at[1, step])
        sums = s_send[step, c]
        for d in range(clus - 1):
            sums = sums + s_recv[step, d]
        masked = jnp.concatenate(
            [jnp.where((lane >= s * rank) & (lane < (s + 1) * rank), sums, 0.0) for s in range(clusters)], axis=0)
        both = jnp.dot(jnp.concatenate(split(masked), axis=0), row_v[...], preferred_element_type=F32)
        part = both[: clusters * rows] + both[clusters * rows :] + jnp.concatenate(near, axis=0)
        n_send[step] = part.astype(WIRE)

        def share(e):
            send(n_send.at[step], n_recv.at[step, e - 1], n_sems.at[0, step], n_sems.at[1, step],
                 {"clus": c, "pair": lax.rem(p + e, pairs)})

        each(1, pairs, share)
        scaled = jnp.concatenate([coeff[degree] * rhs[:, s * leaf : (s + 1) * leaf] for s in range(clusters)], axis=0)

        @pl.when(step < degree_top - 1)
        def _():
            @pl.when(step == 0)
            def _():
                for d in range(2):
                    drain(rq_recv.at[d], rq_sems.at[1, d])

            with_rhs = part + jnp.where(p == 0, 1.0, 0.0) * scaled
            for s in range(clusters):
                held[s] = with_rhs[s * rows : (s + 1) * rows]

            def answer(i):
                d = lax.div(i, pairs)
                e = lax.rem(i, pairs)
                parts = []
                for u in range(CAP):
                    total = jnp.zeros((rows, leaf), F32)
                    for s in range(clusters):
                        weight = rq_recv[d, e, u * clusters + s : u * clusters + s + 1, :]
                        weight = jnp.concatenate([weight] * (leaf // LANES), axis=1)
                        total = total + weight * held[s]
                    parts.append(total)
                sel_send[step, d, e] = jnp.concatenate(parts, axis=0).astype(WIRE)
                there = jnp.where(d == 0, down, up)
                device = {"clus": there, "pair": lax.rem(p + pairs - e, pairs)}
                send(sel_send.at[step, d, e], sel_recv.at[step, 1 - d, e],
                     sel_sems.at[0, step, d], sel_sems.at[1, step, 1 - d], device)

            each(0, 2 * pairs, answer)

        total = part + scaled
        drain(n_recv.at[step], n_sems.at[1, step])
        for e in range(pairs - 1):
            total = total + n_recv[step, e].astype(F32)
        for s in range(clusters):
            result = total[s * rows : (s + 1) * rows]
            out[:, s * leaf : (s + 1) * leaf] = result
            xs[s] = result.astype(BF16).astype(F32)
        return unused

    lax.fori_loop(0, degree_top, product, 0)

    for d in range(2):
        drain(x0_send, x0_sems.at[0, d])
        drain(rq_recv.at[d], rq_sems.at[0, d])
    for step in range(degree_top):
        drain(s_recv.at[step], s_sems.at[0, step])
        drain(n_recv.at[step], n_sems.at[0, step])
        if step < degree_top - 1:
            for d in range(2):
                drain(sel_send.at[step, d], sel_sems.at[0, step, d])


def shards(
    clus, pairs, rhs_field, coefficients, near_blocks, near_tgt, near_src, row_basis, col_basis, far_src, far_tgt
):
    rows = rhs_field.shape[0]
    clusters, rank, leaf = row_basis.shape
    near_count, far_count = near_blocks.shape[0], col_basis.shape[0]
    degree_top = coefficients.shape[0] - 1
    chunk = clusters * rank
    sizes = (clus, pairs, clusters, rows, leaf, rank, near_count, far_count, degree_top)
    hbm = pl.BlockSpec(memory_space=pltpu.HBM)
    fields = clusters * rows
    rounds = degree_top
    return pl.pallas_call(
        functools.partial(kernel, sizes),
        out_shape=jax.ShapeDtypeStruct(rhs_field.shape, F32),
        in_specs=[hbm] * 9,
        out_specs=pl.BlockSpec(memory_space=pltpu.VMEM),
        scratch_shapes=[
            pltpu.SMEM(coefficients.shape, F32),
            pltpu.SMEM(near_tgt.shape, jnp.int32),
            pltpu.SMEM(near_src.shape, jnp.int32),
            pltpu.SMEM(far_src.shape, jnp.int32),
            pltpu.SMEM(far_tgt.shape, jnp.int32),
            pltpu.VMEM(rhs_field.shape, F32),
            pltpu.VMEM(near_blocks.shape, BF16),
            pltpu.VMEM((chunk, leaf), BF16),
            pltpu.VMEM((far_count * rank, leaf), BF16),
            pltpu.VMEM((clusters + 2 * CAP, rows, leaf), F32),
            pltpu.VMEM((fields, leaf), BF16),
            pltpu.VMEM((2, fields, leaf), BF16),
            pltpu.VMEM((2, clusters, rows, leaf), F32),
            pltpu.VMEM((2, CAP * clusters, LANES), F32),
            pltpu.VMEM((2, pairs, CAP * clusters, LANES), F32),
            pltpu.VMEM((far_count * rank // LANES, rows, LANES), jnp.int32),
            pltpu.VMEM((clusters, rows, leaf), F32),
            pltpu.VMEM((far_count * rank, clus * chunk), BF16),
            pltpu.VMEM((rounds, clus, rows, chunk), F32),
            pltpu.VMEM((rounds, clus - 1, rows, chunk), F32),
            pltpu.VMEM((rounds, fields, leaf), WIRE),
            pltpu.VMEM((rounds, pairs - 1, fields, leaf), WIRE),
            pltpu.VMEM((rounds - 1, 2, pairs, CAP * rows, leaf), WIRE),
            pltpu.VMEM((rounds - 1, 2, pairs, CAP * rows, leaf), WIRE),
            pltpu.SMEM((near_count,), jnp.int32),
            pltpu.SemaphoreType.DMA((9,)),
            pltpu.SemaphoreType.DMA((2, 2)),
            pltpu.SemaphoreType.DMA((2, 2)),
            pltpu.SemaphoreType.DMA((2, rounds)),
            pltpu.SemaphoreType.DMA((2, rounds)),
            pltpu.SemaphoreType.DMA((2, rounds - 1, 2)),
        ],
        compiler_params=pltpu.CompilerParams(
            collective_id=0, has_side_effects=True, vmem_limit_bytes=63 * 1024 * 1024
        ),
        name="horner",
    )(
        coefficients, near_tgt, near_src, far_src, far_tgt, rhs_field,
        near_blocks, row_basis.reshape(chunk, leaf), col_basis.reshape(far_count * rank, leaf),
    )


def solution(mesh):
    return jax.shard_map(
        functools.partial(shards, mesh.shape["clus"], mesh.shape["pair"]),
        mesh=mesh,
        in_specs=(
            P("rhs", ("groups", "clus")),
            P(),
            P(("groups", "clus", "pair"), None, None),
            P(("groups", "clus", "pair")),
            P(("groups", "clus", "pair")),
            P(("groups", "clus"), None, None),
            P(("groups", "clus", "pair"), None, None),
            P(("groups", "clus", "pair")),
            P(("groups", "clus", "pair")),
        ),
        out_specs=P("rhs", ("groups", "clus")),
        check_vma=False,
    )
```

profile of v0, /device:TPU:0, one launch (start us, length us, event | category | flops | bytes accessed | tf_op | source)
XLA Modules:
  0.0 30.2 jit_solution(10412029302582291072)
XLA Ops:
  0.0 28.7 %horner.1 = f32[8,2048]{1,0:T(8,128)} custom-call(f32[4]{0:T(128)} %coeff_h.1, s32[16]{0:T(128)} %near_tgt_h.1, s32[16]{0:T(128)} %near_src_h.1, s32[64]{0:T(128)} %far_src_h.1, s32[64]{0:T(128)} %far_tgt_h.1, f32[8,2048]{1,0:T(8,128)} %rhs_h.1, bf16[16,256,256]{2,1,0:T(8,128)(2,1)} %near_h.1, bf16[128,256]{1,0:T(8,128)(2,1)} %bitcast.3, ...), custom_call_target="tpu_custom_call" | custom-call | tf_op jit(solution)/shard_map/horner/pallas_call | solution.py:282
  28.7 1.5 %copy.11 = f32[8,2048]{1,0:T(8,128)} copy(f32[8,2048]{1,0:T(8,128)} %horner.1) | data formatting | bytes 131072
where the time goes:
time: 30.4 us; the launch traced here: 30.2 us
  Pallas kernels  28.7 us (94%)
  local copies, waits for them, and re-layouts  1.47 us (5%)
    pallas_call x1, Pallas kernels, shards(): pl.pallas_call(functools.partial(kernel, sizes), out_shape=jax.ShapeDtype...  28.7 us
    unnamed x1, local copies, waits for them, and re-layouts  1.47 us

commit v1 on v0

--- a/solution.py
+++ b/solution.py
@@ -29,8 +29,8 @@
     sizes, coeff_h, near_tgt_h, near_src_h, far_src_h, far_tgt_h, rhs_h, near_h, row_h, col_h, out,
     coeff, near_tgt, near_src, far_src, far_tgt, rhs, near_v, row_v, col_v,
     xs, x0_send, x0_recv, x0_wide, rq_send, rq_recv,
-    src_lane, held, fold, s_send, s_recv, n_send, n_recv, sel_send, sel_recv, index_s,
-    load_sem, x0_sems, rq_sems, s_sems, n_sems, sel_sems,
+    u_recv, far_side, src_lane, held, fold, s_send, s_recv, n_send, n_recv, sel_send, sel_recv, index_s,
+    load_sem, x0_sems, u_sems, rq_sems, s_sems, n_sems, sel_sems,
 ):
     clus, pairs, clusters, rows, leaf, rank, near_count, far_count, degree_top = sizes
     group = clus * pairs
@@ -108,6 +108,9 @@
             device = {"clus": beside[d], "pair": lax.rem(p + e, pairs)}
             send(rq_send.at[d], rq_recv.at[1 - d, e], rq_sems.at[0, d], rq_sems.at[1, 1 - d], device)
         each(0, pairs, ask)
+    loads[7].wait()
+    for d in range(2):
+        send(row_v, u_recv.at[1 - d], u_sems.at[0, d], u_sems.at[1, 1 - d], {"clus": beside[d], "pair": p})
 
     lane = lax.broadcasted_iota(jnp.int32, (rows, LANES), 1)
     per_tile = LANES // rank
@@ -130,7 +133,6 @@
 
     lax.fori_loop(0, far_count, place_block, 0, unroll=2)
     loads[6].wait()
-    loads[7].wait()
 
     contract_last = (((1,), (1,)), ((), ()))
     tile_lanes = far_count // per_tile
@@ -151,15 +153,15 @@
         coef = jnp.concatenate(parts, axis=1)
         both = jnp.dot(jnp.concatenate(split(coef), axis=0), fold[...], preferred_element_type=F32)
         mine = both[:rows] + both[rows:]
+        chunks = [mine[:, i * chunk : (i + 1) * chunk] for i in range(clus)]
         for i in range(clus):
-            s_send[step, i] = mine[:, i * chunk : (i + 1) * chunk]
+            s_send[step, i] = jnp.concatenate([chunks[(i + k) % clus] for k in (-1, 0, 1)], axis=0)
 
         def spread(d):
-            there = lax.rem(c + d, clus)
-            send(s_send.at[step, there], s_recv.at[step, d - 1], s_sems.at[0, step], s_sems.at[1, step],
-                 {"clus": there, "pair": p})
-
-        each(1, clus, spread)
+            device = peer(d)
+            send(s_send.at[step, device["clus"]], s_recv.at[step, d - 1], s_sems.at[0, step], s_sems.at[1, step], device)
+
+        each(1, group, spread)
 
         @pl.when(step == 0)
         def _():
@@ -176,8 +178,8 @@
         def _():
             for d in range(2):
                 drain(sel_recv.at[step - 1, d], sel_sems.at[1, step - 1, d])
-                value = sel_recv[step - 1, d, 0].astype(F32)
-                for e in range(1, pairs):
+                value = far_side[d]
+                for e in range(pairs):
                     value = value + sel_recv[step - 1, d, e].astype(F32)
                 for u in range(CAP):
                     xs[clusters + d * CAP + u] = value[u * rows : (u + 1) * rows].astype(BF16).astype(F32)
@@ -197,14 +199,7 @@
             0, near_count // NEAR_UNROLL, near_block,
             tuple(jnp.zeros((rows, leaf), F32) for s in range(clusters)))
 
-        drain(s_recv.at[step], s_sems.at[1, step])
-        sums = s_send[step, c]
-        for d in range(clus - 1):
-            sums = sums + s_recv[step, d]
-        masked = jnp.concatenate(
-            [jnp.where((lane >= s * rank) & (lane < (s + 1) * rank), sums, 0.0) for s in range(clusters)], axis=0)
-        both = jnp.dot(jnp.concatenate(split(masked), axis=0), row_v[...], preferred_element_type=F32)
-        part = both[: clusters * rows] + both[clusters * rows :] + jnp.concatenate(near, axis=0)
+        part = jnp.concatenate(near, axis=0)
         n_send[step] = part.astype(WIRE)
 
         def share(e):
@@ -244,7 +239,24 @@
 
             each(0, 2 * pairs, answer)
 
-        total = part + scaled
+        drain(s_recv.at[step], s_sems.at[1, step])
+        sums = lax.fori_loop(0, group - 1, lambda d, t: t + s_recv[step, d], s_send[step, c], unroll=group <= 8)
+
+        def apply(sums, places, basis):
+            masked = jnp.concatenate(
+                [jnp.where((lane >= s * rank) & (lane < (s + 1) * rank), sums, 0.0) for s in places], axis=0)
+            both = jnp.dot(jnp.concatenate(split(masked), axis=0), basis, preferred_element_type=F32)
+            return both[: len(places) * rows] + both[len(places) * rows :]
+
+        @pl.when(step == 0)
+        def _():
+            for d in range(2):
+                drain(u_recv.at[d], u_sems.at[1, d])
+
+        for d in range(2):
+            around = sums[2 * d * rows : (2 * d + 1) * rows]
+            far_side[d] = apply(around, wanted[d * CAP : (d + 1) * CAP], u_recv[d])
+        total = part + scaled + apply(sums[rows : 2 * rows], range(clusters), row_v[...])
         drain(n_recv.at[step], n_sems.at[1, step])
         for e in range(pairs - 1):
             total = total + n_recv[step, e].astype(F32)
@@ -258,6 +270,7 @@
 
     for d in range(2):
         drain(x0_send, x0_sems.at[0, d])
+        drain(row_v, u_sems.at[0, d])
         drain(rq_recv.at[d], rq_sems.at[0, d])
     for step in range(degree_top):
         drain(s_recv.at[step], s_sems.at[0, step])
@@ -300,17 +313,20 @@
             pltpu.VMEM((2, clusters, rows, leaf), F32),
             pltpu.VMEM((2, CAP * clusters, LANES), F32),
             pltpu.VMEM((2, pairs, CAP * clusters, LANES), F32),
+            pltpu.VMEM((2, chunk, leaf), BF16),
+            pltpu.VMEM((2, CAP * rows, leaf), F32),
             pltpu.VMEM((far_count * rank // LANES, rows, LANES), jnp.int32),
             pltpu.VMEM((clusters, rows, leaf), F32),
             pltpu.VMEM((far_count * rank, clus * chunk), BF16),
-            pltpu.VMEM((rounds, clus, rows, chunk), F32),
-            pltpu.VMEM((rounds, clus - 1, rows, chunk), F32),
+            pltpu.VMEM((rounds, clus, 3 * rows, chunk), F32),
+            pltpu.VMEM((rounds, clus * pairs - 1, 3 * rows, chunk), F32),
             pltpu.VMEM((rounds, fields, leaf), WIRE),
             pltpu.VMEM((rounds, pairs - 1, fields, leaf), WIRE),
             pltpu.VMEM((rounds - 1, 2, pairs, CAP * rows, leaf), WIRE),
             pltpu.VMEM((rounds - 1, 2, pairs, CAP * rows, leaf), WIRE),
             pltpu.SMEM((near_count,), jnp.int32),
             pltpu.SemaphoreType.DMA((9,)),
+            pltpu.SemaphoreType.DMA((2, 2)),
             pltpu.SemaphoreType.DMA((2, 2)),
             pltpu.SemaphoreType.DMA((2, 2)),
             pltpu.SemaphoreType.DMA((2, rounds)),

time: 30.4 us -> 28.1 us (0.924)
  Pallas kernels: 28.7 us -> 26.5 us
    pallas_call x1, Pallas kernels: 28.7 us -> 26.5 us  [shards(): pl.pallas_call(functools.partial(kernel, sizes), out_shape=jax.ShapeDtype...]
where the time goes in v1:
time: 28.1 us; the launch traced here: 28 us
  Pallas kernels  26.5 us (94%)
  local copies, waits for them, and re-layouts  1.47 us (5%)
    pallas_call x1, Pallas kernels, shards(): pl.pallas_call(functools.partial(kernel, sizes), out_shape=jax.ShapeDtype...  26.5 us
    unnamed x1, local copies, waits for them, and re-layouts  1.47 us

profile of v1, /device:TPU:0, one launch (start us, length us, event | category | flops | bytes accessed | tf_op | source)
XLA Modules:
  0.0 28.0 jit_solution(4048473567549948849)
XLA Ops:
  0.0 26.5 %horner.1 = f32[8,2048]{1,0:T(8,128)} custom-call(f32[4]{0:T(128)} %coeff_h.1, s32[16]{0:T(128)} %near_tgt_h.1, s32[16]{0:T(128)} %near_src_h.1, s32[64]{0:T(128)} %far_src_h.1, s32[64]{0:T(128)} %far_tgt_h.1, f32[8,2048]{1,0:T(8,128)} %rhs_h.1, bf16[16,256,256]{2,1,0:T(8,128)(2,1)} %near_h.1, bf16[128,256]{1,0:T(8,128)(2,1)} %bitcast.3, ...), custom_call_target="tpu_custom_call" | custom-call | tf_op jit(solution)/shard_map/horner/pallas_call | solution.py:295
  26.5 1.5 %copy.11 = f32[8,2048]{1,0:T(8,128)} copy(f32[8,2048]{1,0:T(8,128)} %horner.1) | data formatting | bytes 131072
